TPU v7x, 512 devices: a whole 4x4x16 slice. The times are simulated.
512 devices in a mesh: row: 128 (over x, z, y_hi), ch: 4 (over y_lo, core).
Axes of the slice: x: 4, y: 4 (y_hi: 2, y_lo: 2; y = y_hi * 2 + y_lo), z: 16, core: 2. Of those that a mesh axis runs over, the one named last changes fastest.
Arguments:
- pair_rep: bfloat16 [128, 128, 128], P('ch', 'row'), may hold values from -6 to 6
- residue_mask: int32 [128], replicated, may hold values 0 or 1
- chain_ids: int32 [128], replicated, may hold values from 0 to 3, never falling along the last dimension, each value on 1 to 64 neighbouring positions
- in_gain: float32 [2, 128], replicated, may hold values from 0.5 to 1.5
- in_bias: float32 [2, 128], replicated, may hold values from -3 to 3
- w_proj: bfloat16 [2, 128, 4, 128], P(None, None, None, 'ch'), may hold values from -0.5 to 0.5
- w_gate: bfloat16 [2, 128, 128], P(None, None, 'ch'), may hold values from -0.5 to 0.5
- pair_bias: float32 [2, 128], P(None, 'ch'), may hold values from -4 to 4
- out_gain: float32 [2, 128], P(None, 'ch'), may hold values from 0.5 to 1.5
- out_bias: float32 [2, 128], P(None, 'ch'), may hold values from -3 to 3
- w_out: bfloat16 [2, 128, 128], P(None, 'ch'), may hold values from -0.5 to 0.5
Outputs:
- pair_out: bfloat16 [128, 128, 128], P('ch', 'row')
Inputs may be any that keep to these rules, and one draw needn't show every extreme that they name: `chain_ids`: chain numbers never fall along the residues; each chain has 1 to 64 residues.
All inputs are finite; a program needn't handle non-finite values.
Results may differ from a plain program's by a relative error of at most 0.013.
Values may be sent and summed in bfloat16 or wider, within the bound.
No kernel may reach another device: no remote copies, remote signals or barrier semaphores. Data moves between devices by JAX's collectives and lax.ppermute only.
A program may use at most 64 MiB of HBM per device.

v0:
```python
import jax
import jax.numpy as jnp
from jax import lax
from jax.sharding import Mesh, PartitionSpec as P

epsilon = 1e-05
bf16 = jnp.bfloat16
f32 = jnp.float32
ROW = ("x", "z", "yh")
PLANE = ("x", "yh", "ch")


def norm(v, gain, bias):
    mean = jnp.mean(v, axis=0)
    var = jnp.mean(v * v, axis=0) - mean * mean
    return ((v - mean) * lax.rsqrt(var + epsilon) * gain[:, None] + bias[:, None]).astype(bf16)


def body(
    pair_rep,
    residue_mask,
    chain_ids,
    in_gain,
    in_bias,
    w_proj,
    w_gate,
    pair_bias,
    out_gain,
    out_bias,
    w_out,
):
    ix, iz, iyh, q = (lax.axis_index(a) for a in ("x", "z", "yh", "ch"))
    row = (ix * 16 + iz) * 2 + iyh
    me = ix * 8 + iyh * 4 + q
    zfull = lax.all_gather(pair_rep[:, 0, :], "ch", axis=0, tiled=True)
    zfull, residue_mask, chain_ids, in_gain, in_bias = lax.optimization_barrier(
        (zfull, residue_mask, chain_ids, in_gain, in_bias)
    )
    mask = residue_mask.astype(f32)
    n0 = norm(zfull.astype(f32), in_gain[0], in_bias[0])
    p0 = jnp.einsum("ck,cpd->pdk", n0, w_proj[0], preferred_element_type=f32)
    pm = mask[row] * mask
    left = (jax.nn.sigmoid(p0[0]) * p0[1] * pm).astype(bf16).reshape(8, 4, 128)
    right = (jax.nn.sigmoid(p0[2]) * p0[3] * pm).astype(bf16).reshape(8, 4, 128)
    zt = lax.dynamic_index_in_dim(zfull.T.reshape(4, 8, 4, 128), q, 2, keepdims=False)
    zt = zt.transpose(1, 0, 2)
    send = jnp.stack([left, right, zt], axis=1).reshape(4, 1, 2, 3, 4, 128)
    send = jnp.broadcast_to(send, (4, 16, 2, 3, 4, 128)).reshape(128, 3, 4, 128)
    got = lax.all_to_all(send, ROW, 0, 0, tiled=True)
    w_gate2 = w_gate.transpose(1, 0, 2).reshape(2, 64, 64).transpose(1, 0, 2).reshape(64, 128)
    packed = jnp.concatenate([w_proj[1].reshape(128, 128), w_gate2, w_out.reshape(64, 128)], axis=0)
    packed = lax.all_gather(packed, "ch", axis=0)
    small = lax.all_gather(jnp.concatenate([pair_bias, out_gain, out_bias], axis=0), "ch", axis=0)
    wp1 = packed[:, :128].reshape(4, 128, 4, 32).transpose(1, 2, 0, 3).reshape(128, 4, 128)
    wg = packed[:, 128:192].reshape(4, 64, 2, 2, 32).transpose(3, 2, 1, 0, 4).reshape(2, 128, 128)
    wo = packed[:, 192:].reshape(4, 2, 32, 128)
    pbias = small[:, 0:2].transpose(1, 0, 2).reshape(2, 128)
    og, ob = (small[:, 2:4], small[:, 4:6])
    x0 = jnp.einsum("jdk,idk->dji", got[:, 1], got[:, 0], preferred_element_type=f32).astype(bf16)
    x0 = x0.reshape(4, 4, 32, 128).transpose(2, 0, 1, 3).reshape(32, 4, 512)
    x0 = lax.all_to_all(x0, PLANE, 0, 0, tiled=True).reshape(128, 512).astype(f32)

    def reorder(w):
        return w.reshape(4, 8, 4, *w.shape[2:]).swapaxes(0, 1).reshape(128, *w.shape[2:])

    cols = jnp.arange(4) * 32 + me
    same = (chain_ids[cols][:, None] == chain_ids[None, :]).astype(f32).reshape(512)
    pm1 = (mask[cols][:, None] * mask[None, :]).reshape(512)
    xn = norm(x0, reorder(og[:, 0]), reorder(ob[:, 0]))
    y = jnp.einsum("dp,dc->cp", xn, reorder(wo[:, 0]), preferred_element_type=f32)
    zp = got[:, 2].transpose(2, 1, 0).reshape(128, 512).astype(f32)
    nz = norm(zp, in_gain[0], in_bias[0])
    gate = jax.nn.sigmoid(
        jnp.einsum("cp,cd->dp", nz, wg[0], preferred_element_type=f32) + pbias[0][:, None] * same
    )
    z1 = (zp + gate * y).astype(bf16)
    n1 = norm(z1.astype(f32), in_gain[1], in_bias[1])
    p1 = jnp.einsum("cp,cxd->xdp", n1, wp1, preferred_element_type=f32)
    left1 = (jax.nn.sigmoid(p1[0]) * p1[1] * pm1).astype(bf16)
    right1 = (jax.nn.sigmoid(p1[2]) * p1[3] * pm1).astype(bf16)
    gate1 = jax.nn.sigmoid(
        jnp.einsum("cp,cd->dp", n1, wg[1], preferred_element_type=f32) + pbias[1][:, None] * same
    ).astype(bf16)
    zg = jnp.stack([z1, gate1]).reshape(2, 4, 32, 4, 4, 16, 2)
    zg = lax.dynamic_index_in_dim(zg, iz, 5, keepdims=False)
    zg = zg.transpose(4, 5, 1, 0, 3, 2).reshape(32, 4, 64)
    send = jnp.concatenate(
        [left1.reshape(32, 4, 512), right1.reshape(32, 4, 512), zg, jnp.zeros((32, 4, 64), bf16)],
        axis=2,
    )
    got = lax.all_to_all(send, PLANE, 0, 0, tiled=True)
    l1 = lax.dynamic_slice_in_dim(got[:, :, :512], iz * 2, 2, 0).reshape(2, 4, 4, 128)
    r1 = got[:, :, 512:1024].reshape(32, 4, 4, 128)
    x1 = jnp.einsum("ydxk,mdtk->xydtm", l1, r1, preferred_element_type=f32).astype(bf16)
    x1 = jnp.broadcast_to(x1.reshape(8, 1, 4, 128), (8, 4, 4, 128)).reshape(32, 4, 128)
    x1 = lax.all_to_all(x1, PLANE, 0, 0, tiled=True).reshape(128, 128).astype(f32)
    xn = norm(x1, og[:, 1].reshape(128), ob[:, 1].reshape(128))
    wo1 = lax.dynamic_slice_in_dim(wo[:, 1].reshape(128, 128), q * 32, 32, 1)
    y = jnp.einsum("dp,dc->cp", xn, wo1, preferred_element_type=f32)
    zg = (
        got[:, :, 1024:1088]
        .reshape(32, 2, 4, 32)
        .transpose(1, 3, 2, 0)
        .reshape(2, 32, 128)
        .astype(f32)
    )
    return (zg[0] + zg[1] * y).astype(bf16)[:, None, :]


def solution(mesh):
    fine = Mesh(mesh.devices.reshape(4, 16, 2, 4), ("x", "z", "yh", "ch"))
    return jax.shard_map(
        body,
        mesh=fine,
        in_specs=(
            P("ch", ROW, None),
            P(),
            P(),
            P(),
            P(),
            P(None, None, None, "ch"),
            P(None, None, "ch"),
            P(None, "ch"),
            P(None, "ch"),
            P(None, "ch"),
            P(None, "ch", None),
        ),
        out_specs=P("ch", ROW, None),
        check_vma=False,
    )
```

profile of v0, /device:TPU:1, one launch (start us, length us, event | category | flops | bytes accessed | tf_op | source)
XLA Modules:
  0.0 107.9 jit_solution(16931430102296169060)
XLA Ops:
  0.0 0.7 copy-done.4
  0.7 11.9 %all-gather.1 = bf16[128,1,128]{2,0,1:T(8,128)(2,1)S(1)} all-gather(bf16[32,1,128]{2,0,1:T(8,128)(2,1)S(1)} %copy-done.4), channel_id=3, replica_groups=mesh['x'=4,'z'=16,'yh'=2,'ch'=4] {'ch'}, dimensions={0}, use_global_device_ids=true | all-gather | bytes 40960 | tf_op jit(solution)/shard_map/all_gather | solution.py:35
  12.7 0.7 copy-done.10
  13.4 0.6 dynamic_slice.17
  13.9 0.6 broadcast_multiply_fusion.3
  14.6 0.1 convert_reduce_fusion.2
  14.8 0.6 copy-done.8
  15.4 0.2 fusion.47
  15.8 0.8 broadcast_in_dim.13
  16.7 16.9 %all-to-all-start = ((bf16[128,3,4,128]{3,2,1,0:T(4,128)(2,1)}), bf16[128,3,4,128]{3,2,1,0:T(4,128)(2,1)S(1)}, u32[]{:S(2)}, u32[]{:S(2)}) async-start(bf16[128,3,4,128]{3,2,1,0:T(4,128)(2,1)} %bitcast.25), calls=%async_computation | async-start | bytes 786432 | tf_op jit(solution)/shard_map/all_to_all | solution.py:49
  33.6 0.7 copy-done.5
  34.3 5.4 %all-gather.3 = f32[4,6,32]{2,1,0:T(8,128)S(1)} all-gather(f32[1,6,32]{2,1,0:T(8,128)S(1)} %maximum_bitcast_fusion.1), channel_id=4, replica_groups=mesh['x'=4,'z'=16,'yh'=2,'ch'=4] {'ch'}, dimensions={0}, use_global_device_ids=true | all-gather | bytes 3840 | tf_op jit(solution)/shard_map/all_gather | solution.py:53
  40.0 0.6 gather_fusion.1
  40.6 0.6 gather_fusion
  41.4 0.7 copy-done.3
  42.3 6.4 %all-gather = bf16[1024,128]{0,1:T(8,128)(2,1)S(1)} all-gather(bf16[256,128]{0,1:T(8,128)(2,1)S(1)} %pad_maximum_fusion), channel_id=2, replica_groups=mesh['x'=4,'z'=16,'yh'=2,'ch'=4] {'ch'}, dimensions={0}, use_global_device_ids=true | all-gather | bytes 327680 | tf_op jit(solution)/shard_map/all_gather | solution.py:52
  48.8 0.2 copy.242
  49.0 0.1 copy.251
  49.7 0.1 copy.243
  50.0 10.7 %all-to-all-done = bf16[128,3,4,128]{3,2,1,0:T(4,128)(2,1)S(1)} async-done(((bf16[128,3,4,128]{3,2,1,0:T(4,128)(2,1)}), bf16[128,3,4,128]{3,2,1,0:T(4,128)(2,1)S(1)}, u32[]{:S(2)}, u32[]{:S(2)}) %all-to-all-start) | async-done | bytes 393248 | tf_op jit(solution)/shard_map/all_to_all | solution.py:49
  60.7 0.1 fusion.69
  60.8 0.2 bitcast_reduce_fusion
  61.1 0.2 convolution_convert_fusion
  61.4 0.7 copy.257
  62.2 7.9 %all-to-all-start.1 = ((bf16[32,4,512]{2,1,0:T(4,128)(2,1)}), bf16[32,4,512]{2,1,0:T(4,128)(2,1)S(1)}, u32[]{:S(2)}, u32[]{:S(2)}) async-start(bf16[32,4,512]{2,1,0:T(4,128)(2,1)} %copy.257), calls=%async_computation.1 | async-start | bytes 262144 | tf_op jit(solution)/shard_map/all_to_all | solution.py:61
  70.0 0.1 copy.280
  70.2 0.2 fusion.35
  70.4 0.2 fusion.8
  70.6 7.1 %all-to-all-done.1 = bf16[32,4,512]{2,1,0:T(4,128)(2,1)S(1)} async-done(((bf16[32,4,512]{2,1,0:T(4,128)(2,1)}), bf16[32,4,512]{2,1,0:T(4,128)(2,1)S(1)}, u32[]{:S(2)}, u32[]{:S(2)}) %all-to-all-start.1) | async-done | bytes 131104 | tf_op jit(solution)/shard_map/all_to_all | solution.py:61
  77.7 0.1 convert_reduce_fusion.1
  77.9 0.1 fusion.18
  78.1 0.2 convert_reduce_fusion
  78.3 0.1 copy.262
  78.4 0.3 fusion.10
  78.8 0.1 copy.264
  78.9 0.2 stack.18
  79.1 0.2 stack.17
  79.6 0.4 fusion.37
  80.0 0.1 slice_multiply_fusion
  80.4 1.0 concatenate.13
  81.4 3.9 %all-to-all-start.2 = ((bf16[32,4,1152]{2,1,0:T(4,128)(2,1)}), bf16[32,4,1152]{2,1,0:T(4,128)(2,1)S(1)}, u32[]{:S(2)}, u32[]{:S(2)}) async-start(bf16[32,4,1152]{2,1,0:T(4,128)(2,1)} %concatenate.13), calls=%async_computation.2 | async-start | bytes 589824 | tf_op jit(solution)/shard_map/all_to_all | solution.py:91
  85.5 9.3 %all-to-all-done.2 = bf16[32,4,1152]{2,1,0:T(4,128)(2,1)S(1)} async-done(((bf16[32,4,1152]{2,1,0:T(4,128)(2,1)}), bf16[32,4,1152]{2,1,0:T(4,128)(2,1)S(1)}, u32[]{:S(2)}, u32[]{:S(2)}) %all-to-all-start.2) | async-done | bytes 294944 | tf_op jit(solution)/shard_map/all_to_all | solution.py:91
  94.9 0.3 fusion.11
  95.3 0.6 broadcast_in_dim.16
  95.9 3.6 %all-to-all-start.3 = ((bf16[32,4,128]{2,1,0:T(4,128)(2,1)}), bf16[32,4,128]{2,1,0:T(4,128)(2,1)S(1)}, u32[]{:S(2)}, u32[]{:S(2)}) async-start(bf16[32,4,128]{2,1,0:T(4,128)(2,1)} %bitcast.62), calls=%async_computation.3 | async-start | bytes 65536 | tf_op jit(solution)/shard_map/all_to_all | solution.py:96
  99.6 0.1 reshape.410
  100.1 6.8 %all-to-all-done.3 = bf16[32,4,128]{2,1,0:T(4,128)(2,1)S(1)} async-done(((bf16[32,4,128]{2,1,0:T(4,128)(2,1)}), bf16[32,4,128]{2,1,0:T(4,128)(2,1)S(1)}, u32[]{:S(2)}, u32[]{:S(2)}) %all-to-all-start.3) | async-done | bytes 32800 | tf_op jit(solution)/shard_map/all_to_all | solution.py:96
  107.0 0.9 fusion.14
  (87 shorter events, 3.2 us)
Async XLA Ops:
  0.0 0.7 copy-start.4
  12.6 2.1 %copy-start.1 = (bf16[2,128,4,32]{1,3,2,0:T(8,128)(2,1)S(1)}, bf16[2,128,4,32]{1,3,2,0:T(8,128)(2,1)}, u32[]{:S(2)}) copy-start(bf16[2,128,4,32]{1,3,2,0:T(8,128)(2,1)} %param.16) | copy-start | bytes 196612
  12.7 0.7 copy-start.10
  14.7 0.7 copy-start.8
  14.7 0.7 copy-start.9
  16.7 16.9 %copy-start.6 = (f32[2,32]{1,0:T(2,128)S(1)}, f32[2,32]{1,0:T(2,128)}, u32[]{:S(2)}) copy-start(f32[2,32]{1,0:T(2,128)} %param.19) | copy-start | bytes 772
  16.7 16.9 %copy-start.7 = (f32[2,32]{1,0:T(2,128)S(1)}, f32[2,32]{1,0:T(2,128)}, u32[]{:S(2)}) copy-start(f32[2,32]{1,0:T(2,128)} %param.18) | copy-start | bytes 772
  16.7 44.0 %all-to-all-start = ((bf16[128,3,4,128]{3,2,1,0:T(4,128)(2,1)}), bf16[128,3,4,128]{3,2,1,0:T(4,128)(2,1)S(1)}, u32[]{:S(2)}, u32[]{:S(2)}) async-start(bf16[128,3,4,128]{3,2,1,0:T(4,128)(2,1)} %bitcast.25), calls=%async_computation | async-start | bytes 786432 | tf_op jit(solution)/shard_map/all_to_all | solution.py:49
  33.6 0.7 copy-start.5
  39.9 0.7 copy-start
  40.6 0.7 copy-start.2
  41.4 0.7 copy-start.3
  62.2 15.6 %all-to-all-start.1 = ((bf16[32,4,512]{2,1,0:T(4,128)(2,1)}), bf16[32,4,512]{2,1,0:T(4,128)(2,1)S(1)}, u32[]{:S(2)}, u32[]{:S(2)}) async-start(bf16[32,4,512]{2,1,0:T(4,128)(2,1)} %copy.257), calls=%async_computation.1 | async-start | bytes 262144 | tf_op jit(solution)/shard_map/all_to_all | solution.py:61
  81.4 13.4 %all-to-all-start.2 = ((bf16[32,4,1152]{2,1,0:T(4,128)(2,1)}), bf16[32,4,1152]{2,1,0:T(4,128)(2,1)S(1)}, u32[]{:S(2)}, u32[]{:S(2)}) async-start(bf16[32,4,1152]{2,1,0:T(4,128)(2,1)} %concatenate.13), calls=%async_computation.2 | async-start | bytes 589824 | tf_op jit(solution)/shard_map/all_to_all | solution.py:91
  95.9 11.0 %all-to-all-start.3 = ((bf16[32,4,128]{2,1,0:T(4,128)(2,1)}), bf16[32,4,128]{2,1,0:T(4,128)(2,1)S(1)}, u32[]{:S(2)}, u32[]{:S(2)}) async-start(bf16[32,4,128]{2,1,0:T(4,128)(2,1)} %bitcast.62), calls=%async_computation.3 | async-start | bytes 65536 | tf_op jit(solution)/shard_map/all_to_all | solution.py:96
where the time goes:
time: 109 us; the launch traced here: 108 us
  waiting for transfers between devices  33.9 us (31%)
  starting transfers between devices  32.3 us (30%)
  blocking collectives  23.7 us (22%)
  local copies, waits for them, and re-layouts  12.5 us (11%)
  matrix products  2.7 us (2%)
  other arithmetic  2.21 us (2%)
    all_to_all x1, starting transfers between devices, body(): got = lax.all_to_all(send, ROW, 0, 0, tiled=True)  16.9 us
    all_gather x1, blocking collectives, body(): zfull = lax.all_gather(pair_rep[:, 0, :], 'ch', axis=0, tiled=True)  11.9 us
    all_to_all x1, waiting for transfers between devices, body(): got = lax.all_to_all(send, ROW, 0, 0, tiled=True)  10.7 us
    all_to_all x1, waiting for transfers between devices, body(): got = lax.all_to_all(send, PLANE, 0, 0, tiled=True)  9.26 us
    all_to_all x1, starting transfers between devices, body(): lax.all_to_all(x0, PLANE, 0, 0, tiled=True).reshape(128, 512).astype(f32)  7.85 us
    all_to_all x1, waiting for transfers between devices, body(): lax.all_to_all(x0, PLANE, 0, 0, tiled=True).reshape(128, 512).astype(f32)  7.1 us
    all_to_all x1, waiting for transfers between devices, body(): lax.all_to_all(x1, PLANE, 0, 0, tiled=True).reshape(128, 128).astype(f32)  6.79 us
    all_gather x1, blocking collectives, body(): packed = lax.all_gather(packed, 'ch', axis=0)  6.42 us
  transfers between devices with their start and end apart: 4, of which 4 were waited for; matrix products, arithmetic and copies ran while one was open for 4% of the time, Pallas kernels for 0%

commit v1 on v0

--- a/solution.py
+++ b/solution.py
@@ -8,6 +8,13 @@
 f32 = jnp.float32
 ROW = ("x", "z", "yh")
 PLANE = ("x", "yh", "ch")
+
+
+def gather_over(array, name, d):
+    count = lax.axis_size(name)
+    tiles = jnp.stack([array for _ in range(count)])
+    tiles = lax.all_to_all(tiles, name, split_axis=0, concat_axis=0)
+    return jnp.concatenate(tiles, axis=d)
 
 
 def norm(v, gain, bias):
@@ -32,7 +39,7 @@
     ix, iz, iyh, q = (lax.axis_index(a) for a in ("x", "z", "yh", "ch"))
     row = (ix * 16 + iz) * 2 + iyh
     me = ix * 8 + iyh * 4 + q
-    zfull = lax.all_gather(pair_rep[:, 0, :], "ch", axis=0, tiled=True)
+    zfull = gather_over(pair_rep[:, 0, :], "ch", 0)
     zfull, residue_mask, chain_ids, in_gain, in_bias = lax.optimization_barrier(
         (zfull, residue_mask, chain_ids, in_gain, in_bias)
     )

time: 109 us -> 121 us (1.11)
  waiting for transfers between devices: 33.9 us -> 47.7 us
  blocking collectives: 23.7 us -> 11.3 us
  starting transfers between devices: 32.3 us -> 42.4 us
  local copies, waits for them, and re-layouts: 12.5 us -> 13.8 us
    all_to_all x1, waiting for transfers between devices: 10.7 us -> 24.5 us  [body(): got = lax.all_to_all(send, ROW, 0, 0, tiled=True)]
    all_gather x1 -> x0, blocking collectives: 11.9 us -> none  [body(): zfull = lax.all_gather(pair_rep[:, 0, :], 'ch', axis=0, tiled=True)]
    all_to_all x0 -> x1, starting transfers between devices: none -> 10.1 us  [gather_over(): tiles = lax.all_to_all(tiles, name, split_axis=0, concat_axis=0)]
    another operation x0 -> x1, local copies, waits for them, and re-layouts: none -> 1.33 us  [gather_over(): tiles = jnp.stack([array for _ in range(count)])]
    unnamed x23 -> x21, local copies, waits for them, and re-layouts: 3.48 us -> 3.42 us
  transfers between devices with their start and end apart: 4 -> 5, of which waited for: 4 -> 4; matrix products, arithmetic and copies ran while one was open for 4% -> 3% of each run, Pallas kernels for 0% -> 0%
where the time goes in v1:
time: 121 us; the launch traced here: 120 us
  waiting for transfers between devices  47.7 us (39%)
  starting transfers between devices  42.4 us (35%)
  local copies, waits for them, and re-layouts  13.8 us (11%)
  blocking collectives  11.3 us (9%)
  matrix products  2.7 us (2%)
  other arithmetic  2.13 us (2%)
    all_to_all x1, waiting for transfers between devices, body(): got = lax.all_to_all(send, ROW, 0, 0, tiled=True)  24.5 us
    all_to_all x1, starting transfers between devices, body(): got = lax.all_to_all(send, ROW, 0, 0, tiled=True)  16.8 us
    all_to_all x1, starting transfers between devices, gather_over(): tiles = lax.all_to_all(tiles, name, split_axis=0, concat_axis=0)  10.1 us
    all_to_all x1, waiting for transfers between devices, body(): got = lax.all_to_all(send, PLANE, 0, 0, tiled=True)  9.26 us
    all_to_all x1, starting transfers between devices, body(): lax.all_to_all(x0, PLANE, 0, 0, tiled=True).reshape(128, 512).astype(f32)  8 us
    all_to_all x1, waiting for transfers between devices, body(): lax.all_to_all(x0, PLANE, 0, 0, tiled=True).reshape(128, 512).astype(f32)  7.1 us
    all_to_all x1, waiting for transfers between devices, body(): lax.all_to_all(x1, PLANE, 0, 0, tiled=True).reshape(128, 128).astype(f32)  6.79 us
    all_gather x1, blocking collectives, body(): packed = lax.all_gather(packed, 'ch', axis=0)  6.12 us
  transfers between devices with their start and end apart: 5, of which 4 were waited for; matrix products, arithmetic and copies ran while one was open for 3% of the time, Pallas kernels for 0%

profile of v1, /device:TPU:1, one launch (start us, length us, event | category | flops | bytes accessed | tf_op | source)
XLA Modules:
  0.0 120.5 jit_solution(11215278988244412929)
XLA Ops:
  0.0 1.3 %stack.18 = bf16[4,32,128]{2,1,0:T(8,128)(2,1)} broadcast(bf16[32,128]{1,0:T(8,128)(2,1)} %bitcast.174), dimensions={1,2} | broadcast | bytes 40960 | tf_op jit(solution)/shard_map/stack | solution.py:15
  1.3 10.1 %all-to-all-start = ((bf16[4,32,128]{2,1,0:T(8,128)(2,1)}), bf16[4,32,128]{2,1,0:T(8,128)(2,1)S(1)}, u32[]{:S(2)}, u32[]{:S(2)}) async-start(bf16[4,32,128]{2,1,0:T(8,128)(2,1)} %stack.18), calls=%async_computation | async-start | bytes 65536 | tf_op jit(solution)/shard_map/all_to_all | solution.py:16
  11.5 0.7 copy-done.2
  12.3 0.7 copy-done.3
  13.2 6.1 %all-gather = bf16[1024,128]{0,1:T(8,128)(2,1)S(1)} all-gather(bf16[256,128]{0,1:T(8,128)(2,1)S(1)} %pad_maximum_fusion), channel_id=2, replica_groups=mesh['x'=4,'z'=16,'yh'=2,'ch'=4] {'ch'}, dimensions={0}, use_global_device_ids=true | all-gather | bytes 327680 | tf_op jit(solution)/shard_map/all_gather | solution.py:59
  19.3 0.2 copy.236
  19.5 0.6 copy-done.4
  20.2 5.1 %all-gather.2 = f32[4,6,32]{2,1,0:T(8,128)S(1)} all-gather(f32[1,6,32]{2,1,0:T(8,128)S(1)} %maximum_bitcast_fusion.1), channel_id=3, replica_groups=mesh['x'=4,'z'=16,'yh'=2,'ch'=4] {'ch'}, dimensions={0}, use_global_device_ids=true | all-gather | bytes 3840 | tf_op jit(solution)/shard_map/all_gather | solution.py:60
  25.4 0.7 copy-done.9
  26.0 0.6 dynamic_slice.17
  26.6 0.6 broadcast_multiply_fusion.3
  27.4 0.6 copy-done.7
  28.0 0.2 fusion.47
  28.5 0.8 broadcast_in_dim.13
  29.4 16.8 %all-to-all-start.1 = ((bf16[128,3,4,128]{3,2,1,0:T(4,128)(2,1)}), bf16[128,3,4,128]{3,2,1,0:T(4,128)(2,1)S(1)}, u32[]{:S(2)}, u32[]{:S(2)}) async-start(bf16[128,3,4,128]{3,2,1,0:T(4,128)(2,1)} %bitcast.26), calls=%async_computation.1 | async-start | bytes 786432 | tf_op jit(solution)/shard_map/all_to_all | solution.py:56
  46.3 0.1 copy.244
  47.0 0.1 copy.237
  47.2 0.6 gather_fusion.1
  47.9 0.6 gather_fusion
  48.7 24.5 %all-to-all-done.1 = bf16[128,3,4,128]{3,2,1,0:T(4,128)(2,1)S(1)} async-done(((bf16[128,3,4,128]{3,2,1,0:T(4,128)(2,1)}), bf16[128,3,4,128]{3,2,1,0:T(4,128)(2,1)S(1)}, u32[]{:S(2)}, u32[]{:S(2)}) %all-to-all-start.1) | async-done | bytes 393248 | tf_op jit(solution)/shard_map/all_to_all | solution.py:56
  73.2 0.1 fusion.69
  73.3 0.2 bitcast_reduce_fusion
  73.6 0.2 convolution_convert_fusion
  73.9 0.7 copy.250
  74.7 8.0 %all-to-all-start.2 = ((bf16[32,4,512]{2,1,0:T(4,128)(2,1)}), bf16[32,4,512]{2,1,0:T(4,128)(2,1)S(1)}, u32[]{:S(2)}, u32[]{:S(2)}) async-start(bf16[32,4,512]{2,1,0:T(4,128)(2,1)} %copy.250), calls=%async_computation.2 | async-start | bytes 262144 | tf_op jit(solution)/shard_map/all_to_all | solution.py:68
  82.7 0.1 copy.272
  82.8 0.2 fusion.35
  83.0 0.2 fusion.8
  83.3 7.1 %all-to-all-done.2 = bf16[32,4,512]{2,1,0:T(4,128)(2,1)S(1)} async-done(((bf16[32,4,512]{2,1,0:T(4,128)(2,1)}), bf16[32,4,512]{2,1,0:T(4,128)(2,1)S(1)}, u32[]{:S(2)}, u32[]{:S(2)}) %all-to-all-start.2) | async-done | bytes 131104 | tf_op jit(solution)/shard_map/all_to_all | solution.py:68
  90.4 0.1 convert_reduce_fusion.1
  90.5 0.1 fusion.18
  90.7 0.2 convert_reduce_fusion
  90.9 0.1 copy.255
  91.1 0.3 fusion.10
  91.4 0.1 copy.257
  91.5 0.2 stack.22
  91.8 0.2 stack.21
  92.2 0.4 fusion.37
  92.6 0.1 slice_multiply_fusion
  93.0 1.0 concatenate.13
  94.0 3.9 %all-to-all-start.3 = ((bf16[32,4,1152]{2,1,0:T(4,128)(2,1)}), bf16[32,4,1152]{2,1,0:T(4,128)(2,1)S(1)}, u32[]{:S(2)}, u32[]{:S(2)}) async-start(bf16[32,4,1152]{2,1,0:T(4,128)(2,1)} %concatenate.13), calls=%async_computation.3 | async-start | bytes 589824 | tf_op jit(solution)/shard_map/all_to_all | solution.py:98
  98.1 9.3 %all-to-all-done.3 = bf16[32,4,1152]{2,1,0:T(4,128)(2,1)S(1)} async-done(((bf16[32,4,1152]{2,1,0:T(4,128)(2,1)}), bf16[32,4,1152]{2,1,0:T(4,128)(2,1)S(1)}, u32[]{:S(2)}, u32[]{:S(2)}) %all-to-all-start.3) | async-done | bytes 294944 | tf_op jit(solution)/shard_map/all_to_all | solution.py:98
  107.6 0.3 fusion.11
  108.0 0.6 broadcast_in_dim.16
  108.6 3.6 %all-to-all-start.4 = ((bf16[32,4,128]{2,1,0:T(4,128)(2,1)}), bf16[32,4,128]{2,1,0:T(4,128)(2,1)S(1)}, u32[]{:S(2)}, u32[]{:S(2)}) async-start(bf16[32,4,128]{2,1,0:T(4,128)(2,1)} %bitcast.63), calls=%async_computation.4 | async-start | bytes 65536 | tf_op jit(solution)/shard_map/all_to_all | solution.py:103
  112.2 0.1 reshape.416
  112.8 6.8 %all-to-all-done.4 = bf16[32,4,128]{2,1,0:T(4,128)(2,1)S(1)} async-done(((bf16[32,4,128]{2,1,0:T(4,128)(2,1)}), bf16[32,4,128]{2,1,0:T(4,128)(2,1)S(1)}, u32[]{:S(2)}, u32[]{:S(2)}) %all-to-all-start.4) | async-done | bytes 32800 | tf_op jit(solution)/shard_map/all_to_all | solution.py:103
  119.6 0.9 fusion.14
  (87 shorter events, 3.2 us)
Async XLA Ops:
  0.0 11.4 %copy-start.1 = (bf16[2,128,4,32]{1,3,2,0:T(8,128)(2,1)S(1)}, bf16[2,128,4,32]{1,3,2,0:T(8,128)(2,1)}, u32[]{:S(2)}) copy-start(bf16[2,128,4,32]{1,3,2,0:T(8,128)(2,1)} %param.16) | copy-start | bytes 196612
  1.3 24.1 %all-to-all-start = ((bf16[4,32,128]{2,1,0:T(8,128)(2,1)}), bf16[4,32,128]{2,1,0:T(8,128)(2,1)S(1)}, u32[]{:S(2)}, u32[]{:S(2)}) async-start(bf16[4,32,128]{2,1,0:T(8,128)(2,1)} %stack.18), calls=%async_computation | async-start | bytes 65536 | tf_op jit(solution)/shard_map/all_to_all | solution.py:16
  11.4 0.7 copy-start.2
  12.2 0.7 copy-start.3
  19.5 0.7 copy-start.4
  19.5 0.7 copy-start.5
  19.5 0.7 copy-start.6
  25.4 0.7 copy-start.9
  27.3 0.7 copy-start.7
  27.3 0.7 copy-start.8
  29.4 43.8 %all-to-all-start.1 = ((bf16[128,3,4,128]{3,2,1,0:T(4,128)(2,1)}), bf16[128,3,4,128]{3,2,1,0:T(4,128)(2,1)S(1)}, u32[]{:S(2)}, u32[]{:S(2)}) async-start(bf16[128,3,4,128]{3,2,1,0:T(4,128)(2,1)} %bitcast.26), calls=%async_computation.1 | async-start | bytes 786432 | tf_op jit(solution)/shard_map/all_to_all | solution.py:56
  47.2 0.7 copy-start
  74.7 15.7 %all-to-all-start.2 = ((bf16[32,4,512]{2,1,0:T(4,128)(2,1)}), bf16[32,4,512]{2,1,0:T(4,128)(2,1)S(1)}, u32[]{:S(2)}, u32[]{:S(2)}) async-start(bf16[32,4,512]{2,1,0:T(4,128)(2,1)} %copy.250), calls=%async_computation.2 | async-start | bytes 262144 | tf_op jit(solution)/shard_map/all_to_all | solution.py:68
  94.0 13.4 %all-to-all-start.3 = ((bf16[32,4,1152]{2,1,0:T(4,128)(2,1)}), bf16[32,4,1152]{2,1,0:T(4,128)(2,1)S(1)}, u32[]{:S(2)}, u32[]{:S(2)}) async-start(bf16[32,4,1152]{2,1,0:T(4,128)(2,1)} %concatenate.13), calls=%async_computation.3 | async-start | bytes 589824 | tf_op jit(solution)/shard_map/all_to_all | solution.py:98
  108.6 11.0 %all-to-all-start.4 = ((bf16[32,4,128]{2,1,0:T(4,128)(2,1)}), bf16[32,4,128]{2,1,0:T(4,128)(2,1)S(1)}, u32[]{:S(2)}, u32[]{:S(2)}) async-start(bf16[32,4,128]{2,1,0:T(4,128)(2,1)} %bitcast.63), calls=%async_computation.4 | async-start | bytes 65536 | tf_op jit(solution)/shard_map/all_to_all | solution.py:103
